TPU v7x, 32 devices: a whole 2x2x4 slice. The times are simulated.
32 devices in a mesh: groups: 2 (over x), wide: 8 (over z, y), narrow: 2 (over core).
Axes of the slice: x: 2, y: 2, z: 4, core: 2. Of those that a mesh axis runs over, the one named last changes fastest.
Arguments:
- draft_rows: bfloat16 [256, 8192], P(('groups', 'wide'), 'narrow'), parts along dimension 0, may hold values from -6 to 6
- gate_weight: bfloat16 [8192, 4096], P('narrow', 'wide'), may hold values from -0.0625 to 0.0625
- up_weight: bfloat16 [8192, 4096], P('narrow', 'wide'), may hold values from -0.0625 to 0.0625
- down_weight: bfloat16 [4096, 8192], P('wide', 'narrow'), may hold values from -0.09375 to 0.09375
Outputs:
- ffn_out: bfloat16 [256, 8192], P(('groups', 'wide'), 'narrow'), parts along dimension 0
There are 2 independent parts, one for each index of `groups`. A program takes and returns all parts, laid end to end along the dimension named above; an argument that names none is the same for every part. Nothing has to cross between parts.
All inputs are finite; a program needn't handle non-finite values.
Results may differ from a plain program's by a relative error of at most 0.0049.
Values may be sent and summed in bfloat16 or wider, within the bound.
A program may use at most 64 MiB of HBM per device.

v0:
```python
import jax
import jax.numpy as jnp
from jax import lax
from jax.sharding import PartitionSpec as P


def body(draft_rows, gate_weight, up_weight, down_weight):
    hidden_width = gate_weight.shape[1]
    slab_rows = lax.all_gather(draft_rows, "wide", axis=0, tiled=True)
    gate_part = jnp.dot(slab_rows, gate_weight, preferred_element_type=jnp.float32)
    up_part = jnp.dot(slab_rows, up_weight, preferred_element_type=jnp.float32)
    partial_value = jnp.concatenate([gate_part, up_part], axis=1)
    summed = lax.psum(partial_value, "narrow")
    hidden = (jax.nn.silu(summed[:, :hidden_width]) * summed[:, hidden_width:]).astype(jnp.bfloat16)
    products = jnp.dot(hidden, down_weight, preferred_element_type=jnp.float32)
    result = lax.psum_scatter(products, "wide", scatter_dimension=0, tiled=True)
    return result.astype(jnp.bfloat16)


def solution(mesh):
    in_specs = (
        P(("groups", "wide"), "narrow"),
        P("narrow", "wide"),
        P("narrow", "wide"),
        P("wide", "narrow"),
    )
    out_specs = P(("groups", "wide"), "narrow")
    return jax.shard_map(body, mesh=mesh, in_specs=in_specs, out_specs=out_specs, check_vma=False)
```

profile of v0, /device:TPU:1, one launch (start us, length us, event | category | flops | bytes accessed | tf_op | source)
XLA Modules:
  0.0 155.0 jit_solution(15175329129974656912)
XLA Ops:
  6.5 0.0 all-gather.2.cloned.1.call-start
  6.5 0.7 all-gather.2.cloned.1.call-update
  7.3 0.0 all-reduce.2.cloned.1.call-start
  7.3 43.4 %all-gather.2.cloned.1.call-done = bf16[128,4096]{1,0:T(8,128)(2,1)} async-done(((bf16[16,4096]{1,0:T(8,128)(2,1)}), bf16[128,4096]{1,0:T(8,128)(2,1)}) %all-gather.2.cloned.1.call-update) | async-done | bytes 1048592 | tf_op jit(solution)/shard_map/all_gather | solution.py:9
  50.7 0.0 copy-start
  50.8 0.0 copy-start.1
  50.8 3.4 %fusion.6 = f32[128,512]{1,0:T(8,128)S(1)} fusion(bf16[128,4096]{1,0:T(8,128)(2,1)} %all-gather.2.cloned.1.call-done, bf16[4096,512]{1,0:T(8,128)(2,1)} %param.6), kind=kOutput, calls=%fused_computation.7 | convolution fusion | flops 536870912 | bytes 5505024 | tf_op jit(solution)/shard_map/dot_general | solution.py:11
  54.1 0.4 copy-done
  54.5 0.3 copy-done.1
  54.8 0.7 fusion.5
  55.5 0.8 pad_maximum_fusion
  56.3 0.0 all-reduce.2.cloned.1.call-update
  56.4 0.0 reduce-scatter.2.cloned.1.call-start
  56.4 19.0 %all-reduce.2.cloned.1.call-done = f32[128,1024]{1,0:T(8,128)} async-done(((f32[128,1024]{1,0:T(8,128)}), f32[128,1024]{1,0:T(8,128)}) %all-reduce.2.cloned.1.call-update) | async-done | bytes 524304 | tf_op jit(solution)/shard_map/psum | solution.py:13
  75.4 4.4 %fusion.1 = f32[128,4096]{1,0:T(8,128)} fusion(bf16[512,4096]{1,0:T(8,128)(2,1)} %param.7, f32[128,1024]{1,0:T(8,128)} %all-reduce.2.cloned.1.call-done), kind=kOutput, calls=%fused_computation.3 | convolution fusion | flops 537264128 | bytes 6815744 | tf_op jit(solution)/shard_map/dot_general | solution.py:15
  79.8 0.0 reduce-scatter.2.cloned.1.call-update
  79.8 67.0 %reduce-scatter.2.cloned.1.call-done = f32[16,4096]{1,0:T(8,128)} async-done(((f32[128,4096]{1,0:T(8,128)}), f32[16,4096]{1,0:T(8,128)}) %reduce-scatter.2.cloned.1.call-update) | async-done | bytes 262160 | tf_op jit(solution)/shard_map/reduce_scatter | solution.py:16
  146.9 1.6 %convert_element_type.7 = bf16[16,4096]{1,0:T(8,128)(2,1)} convert(f32[16,4096]{1,0:T(8,128)} %reduce-scatter.2.cloned.1.call-done) | non-fusion elementwise | flops 65536 | bytes 393216 | tf_op jit(solution)/shard_map/convert_element_type | solution.py:17
Async XLA Ops:
  6.5 44.2 %all-gather.2.cloned.1.call-start = ((), (), s32[]{:S(2)}) async-start(), calls=%async_computation.1 | async-start | bytes 1179648 | tf_op jit(solution)/shard_map/all_gather | solution.py:9
  7.3 68.1 %all-reduce.2.cloned.1.call-start = ((), (), s32[]{:S(2)}) async-start(), calls=%async_computation.2 | async-start | bytes 1048576 | tf_op jit(solution)/shard_map/psum | solution.py:13
  50.7 3.7 %copy-start = (bf16[4096,512]{1,0:T(8,128)(2,1)S(1)}, bf16[4096,512]{1,0:T(8,128)(2,1)}, u32[]{:S(2)}) copy-start(bf16[4096,512]{1,0:T(8,128)(2,1)} %param.5) | copy-start | bytes 12582916
  50.8 4.0 %copy-start.1 = (bf16[128,4096]{1,0:T(8,128)(2,1)S(1)}, bf16[128,4096]{1,0:T(8,128)(2,1)}, u32[]{:S(2)}) copy-start(bf16[128,4096]{1,0:T(8,128)(2,1)} %all-gather.2.cloned.1.call-done) | copy-start | bytes 3145732
  56.4 90.5 %reduce-scatter.2.cloned.1.call-start = ((), (), s32[]{:S(2)}) async-start(), calls=%async_computation.3 | async-start | bytes 2359296 | tf_op jit(solution)/shard_map/reduce_scatter | solution.py:16
Sparse Core Ops, SparseCore 0:
  9.5 41.2 all-gather.1
  56.5 18.8 all-reduce.1
  80.0 66.8 reduce-scatter.1
where the time goes:
time: 158 us; the launch traced here: 155 us
  waiting for transfers between devices  130 us (82%)
  between operations  13.1 us (8%)
  matrix products  8.53 us (5%)
  other arithmetic  2.44 us (2%)
    reduce_scatter x1, waiting for transfers between devices, body(): result = lax.psum_scatter(products, 'wide', scatter_dimension=0, tiled=True)  67 us
    all_gather x1, waiting for transfers between devices, body(): slab_rows = lax.all_gather(draft_rows, 'wide', axis=0, tiled=True)  43.4 us
    psum x1, waiting for transfers between devices, body(): summed = lax.psum(partial_value, 'narrow')  19 us
    dot_general x1, matrix products, body(): products = jnp.dot(hidden, down_weight, preferred_element_type=jnp.float32)  4.44 us
    dot_general x1, matrix products, body(): up_part = jnp.dot(slab_rows, up_weight, preferred_element_type=jnp.float32)  3.37 us
  transfers between devices with their start and end apart: 3, of which 3 were waited for; matrix products, arithmetic and copies ran while one was open for 0% of the time, Pallas kernels for 0%

commit v1 on v0

v1 whole, which is shorter than its diff:
```python
import functools

import jax
import jax.numpy as jnp
from jax import lax
from jax.experimental import pallas as pl
from jax.experimental.pallas import tpu as pltpu
from jax.sharding import PartitionSpec as P

MESH = pl.DeviceIdType.MESH
COLUMN = 2
DEPTH_CHUNKS = 4
HIDDEN_TILES = 2
OUT_CHUNKS = 8


def kernel(wide, x_hbm, gate_hbm, up_hbm, down_hbm, out_ref,
           xg, gate, up, down, acc, peer, hid, own, y_out, y_in, z_out, z_in,
           w_sem, d_sem, x_sem, zs, zr, ys, yr, ns, nr, rys, ryr, rzs, rzr):
    zn = wide // COLUMN
    rows, width = x_hbm.shape
    half = zn * rows
    units = gate_hbm.shape[1]
    depth = width // DEPTH_CHUNKS
    tile = units // HIDDEN_TILES
    cols = width // OUT_CHUNKS

    me = lax.axis_index("wide")
    z, y = me // COLUMN, lax.rem(me, COLUMN)
    core = lax.axis_index("narrow")
    across = {"wide": z * COLUMN + (1 - y)}
    twin = {"narrow": 1 - core}

    def along(d):
        return {"wide": lax.rem(z + d, zn) * COLUMN + y}

    def local(k):
        part = pl.ds(k * depth, depth)
        return [
            pltpu.make_async_copy(gate_hbm.at[part], gate.at[part], w_sem.at[0, k]),
            pltpu.make_async_copy(up_hbm.at[part], up.at[part], w_sem.at[1, k]),
        ]

    def remote(src, dst, send, recv, to):
        return pltpu.make_async_remote_copy(
            src_ref=src, dst_ref=dst, send_sem=send, recv_sem=recv, device_id=to, device_id_type=MESH)

    mine = pltpu.make_async_copy(x_hbm, xg.at[0], x_sem)
    mine.start()
    for k in range(DEPTH_CHUNKS):
        for copy in local(k):
            copy.start()
    down_copy = pltpu.make_async_copy(down_hbm, down, d_sem)
    down_copy.start()

    barrier = pltpu.get_barrier_semaphore()
    for d in range(1, zn):
        pl.semaphore_signal(barrier, inc=1, device_id=along(d), device_id_type=MESH)
    pl.semaphore_signal(barrier, inc=1, device_id=across, device_id_type=MESH)
    pl.semaphore_signal(barrier, inc=1, device_id=twin, device_id_type=MESH)
    pl.semaphore_wait(barrier, zn + 1)

    def z_copy(k, d):
        part = pl.ds(k * depth, depth)
        return remote(x_hbm.at[:, part], xg.at[zn - d, :, part], zs.at[k, d], zr.at[k, zn - d], along(d))

    def y_copy(k, s):
        part = pl.ds(k * depth, depth)
        src = x_hbm.at[:, part] if s == 0 else xg.at[s, :, part]
        return remote(src, xg.at[zn + s, :, part], ys.at[k, s], yr.at[k, s], across)

    for k in range(DEPTH_CHUNKS):
        y_copy(k, 0).start()
        for d in range(1, zn):
            z_copy(k, d).start()

    def relay(k):
        for s in sorted(range(1, zn), key=lambda s: min(s, zn - s)):
            z_copy(k, zn - s).wait_recv()
            y_copy(k, s).start()

    def twin_copy(t):
        return remote(acc.at[t], peer.at[t], ns.at[t], nr.at[t], twin)

    def project(k):
        for s in range(zn):
            y_copy(k, s).wait_recv()
        for copy in local(k):
            copy.wait()
        part = pl.ds(k * depth, depth)
        x = xg[:, :, part].reshape(2 * half, depth)
        for t in range(HIDDEN_TILES):
            mid = pl.ds(t * tile, tile)
            for i, weight in enumerate((gate, up)):
                value = jnp.dot(x, weight[part, mid], preferred_element_type=jnp.float32)
                place = pl.ds(i * tile, tile)
                if k == 0:
                    acc[t, :, place] = value
                else:
                    acc[t, :, place] += value
            if k == DEPTH_CHUNKS - 1:
                twin_copy(t).start()

    mine.wait()
    for k in range(DEPTH_CHUNKS):
        relay(k)
        if k > 0:
            project(k - 1)
    project(DEPTH_CHUNKS - 1)

    for t in range(HIDDEN_TILES):
        twin_copy(t).wait_recv()
        total = acc[t] + peer[t]
        gate_sum, up_sum = total[:, :tile], total[:, tile:]
        hid[:, pl.ds(t * tile, tile)] = (gate_sum / (1 + jnp.exp(-gate_sum)) * up_sum).astype(jnp.bfloat16)

    down_copy.wait()

    def ry_copy(n):
        return remote(y_out.at[n], y_in.at[n], rys.at[n], ryr.at[n], across)

    def rz_copy(n, d):
        return remote(z_out.at[n, d], z_in.at[n, zn - d], rzs.at[n, d], rzr.at[n, zn - d], along(d))

    for n in range(OUT_CHUNKS):
        products = jnp.dot(hid[...], down[:, pl.ds(n * cols, cols)], preferred_element_type=jnp.float32)
        y_out[n] = products[half:].astype(jnp.bfloat16)
        ry_copy(n).start()
        own[n] = products[:half]

    for n in range(OUT_CHUNKS):
        ry_copy(n).wait_recv()
        for d in range(zn):
            row = pl.ds(d * rows, rows)
            value = own[n, row] + y_in[n, row].astype(jnp.float32)
            if d == 0:
                own[n, row] = value
            else:
                z_out[n, d] = value.astype(jnp.bfloat16)
                rz_copy(n, d).start()

    for n in range(OUT_CHUNKS):
        value = own[n, pl.ds(0, rows)]
        for s in range(1, zn):
            rz_copy(n, zn - s).wait_recv()
            value = value + z_in[n, s].astype(jnp.float32)
        out_ref[:, pl.ds(n * cols, cols)] = value.astype(jnp.bfloat16)

    for k in range(DEPTH_CHUNKS):
        for d in range(zn):
            y_copy(k, d).wait_send()
            if d > 0:
                z_copy(k, d).wait_send()
    for t in range(HIDDEN_TILES):
        twin_copy(t).wait_send()
    for n in range(OUT_CHUNKS):
        ry_copy(n).wait_send()
        for d in range(1, zn):
            rz_copy(n, d).wait_send()


def solution(mesh):
    wide = mesh.shape["wide"]
    zn = wide // COLUMN

    def body(x, gate, up, down):
        rows, width = x.shape
        units = gate.shape[1]
        half, cols, tile = zn * rows, width // OUT_CHUNKS, units // HIDDEN_TILES
        bf16, f32 = jnp.bfloat16, jnp.float32
        dma = pltpu.SemaphoreType.DMA
        return pl.pallas_call(
            functools.partial(kernel, wide),
            out_shape=jax.ShapeDtypeStruct((rows, width), bf16),
            in_specs=[pl.BlockSpec(memory_space=pltpu.HBM)] * 4,
            out_specs=pl.BlockSpec(memory_space=pltpu.VMEM),
            scratch_shapes=[
                pltpu.VMEM((wide, rows, width), bf16),
                pltpu.VMEM(gate.shape, bf16),
                pltpu.VMEM(up.shape, bf16),
                pltpu.VMEM(down.shape, bf16),
                pltpu.VMEM((HIDDEN_TILES, 2 * half, 2 * tile), f32),
                pltpu.VMEM((HIDDEN_TILES, 2 * half, 2 * tile), f32),
                pltpu.VMEM((2 * half, units), bf16),
                pltpu.VMEM((OUT_CHUNKS, half, cols), f32),
                pltpu.VMEM((OUT_CHUNKS, half, cols), bf16),
                pltpu.VMEM((OUT_CHUNKS, half, cols), bf16),
                pltpu.VMEM((OUT_CHUNKS, zn, rows, cols), bf16),
                pltpu.VMEM((OUT_CHUNKS, zn, rows, cols), bf16),
                dma((2, DEPTH_CHUNKS)), dma, dma,
                dma((DEPTH_CHUNKS, zn)), dma((DEPTH_CHUNKS, zn)),
                dma((DEPTH_CHUNKS, zn)), dma((DEPTH_CHUNKS, zn)),
                dma((HIDDEN_TILES,)), dma((HIDDEN_TILES,)),
                dma((OUT_CHUNKS,)), dma((OUT_CHUNKS,)),
                dma((OUT_CHUNKS, zn)), dma((OUT_CHUNKS, zn)),
            ],
            compiler_params=pltpu.CompilerParams(
                collective_id=0, has_side_effects=True, vmem_limit_bytes=56 * 1024 * 1024),
        )(x, gate, up, down)

    in_specs = (
        P(("groups", "wide"), "narrow"),
        P("narrow", "wide"),
        P("narrow", "wide"),
        P("wide", "narrow"),
    )
    out_specs = P(("groups", "wide"), "narrow")
    return jax.shard_map(body, mesh=mesh, in_specs=in_specs, out_specs=out_specs, check_vma=False)
```

time: 158 us -> 45.2 us (0.29); the launches traced: 155 us -> 44.7 us
  waiting for transfers between devices: 130 us -> 0 us
  Pallas kernels: 0 us -> 43.2 us
  between operations: 13.1 us -> 0.01 us
  matrix products: 8.53 us -> 0 us
  other arithmetic: 2.44 us -> 0 us
    reduce_scatter x1 -> x0, waiting for transfers between devices: 67 us -> none  [body(): result = lax.psum_scatter(products, 'wide', scatter_dimension=0, tiled=True)]
    all_gather x1 -> x0, waiting for transfers between devices: 43.4 us -> none  [body(): slab_rows = lax.all_gather(draft_rows, 'wide', axis=0, tiled=True)]
    pallas_call x0 -> x1, Pallas kernels: none -> 43.2 us  [body(): pl.pallas_call(functools.partial(kernel, wide), out_shape=jax.ShapeDtypeS...]
    psum x1 -> x0, waiting for transfers between devices: 19 us -> none  [body(): summed = lax.psum(partial_value, 'narrow')]
    dot_general x3 -> x0, matrix products: 8.53 us -> none  [the longest x1 4.44 us: body(): products = jnp.dot(hidden, down_weight, preferred_element_type=jnp.float32)]
    convert_element_type x1 -> x0, other arithmetic: 1.62 us -> none  [body(): return result.astype(jnp.bfloat16)]
  transfers between devices with their start and end apart: 3 -> 0, of which waited for: 3 -> 0; matrix products, arithmetic and copies ran while one was open for 0% -> 0% of each run, Pallas kernels for 0% -> 0%
where the time goes in v1:
time: 45.2 us; the launch traced here: 44.7 us
  Pallas kernels  43.2 us (96%)
  local copies, waits for them, and re-layouts  1.57 us (3%)
    pallas_call x1, Pallas kernels, body(): pl.pallas_call(functools.partial(kernel, wide), out_shape=jax.ShapeDtypeS...  43.2 us
    unnamed x1, local copies, waits for them, and re-layouts  1.57 us

profile of v1, /device:TPU:1, one launch (start us, length us, event | category | flops | bytes accessed | tf_op | source)
XLA Modules:
  0.0 44.7 jit_solution(14504523305808092963)
XLA Ops:
  0.0 43.2 %shard_map.46 = bf16[16,4096]{1,0:T(8,128)(2,1)} custom-call(bf16[16,4096]{1,0:T(8,128)(2,1)} %x_hbm.1, bf16[4096,512]{1,0:T(8,128)(2,1)} %gate_hbm.1, bf16[4096,512]{1,0:T(8,128)(2,1)} %up_hbm.1, bf16[512,4096]{1,0:T(8,128)(2,1)} %down_hbm.1), custom_call_target="tpu_custom_call" | custom-call | tf_op jit(solution)/shard_map/pallas_call | solution.py:172
  43.2 1.6 %copy.6 = bf16[16,4096]{1,0:T(8,128)(2,1)} copy(bf16[16,4096]{1,0:T(8,128)(2,1)} %shard_map.46) | data formatting | bytes 262144

commit v2 on v1

--- a/solution.py
+++ b/solution.py
@@ -9,19 +9,22 @@
 
 MESH = pl.DeviceIdType.MESH
 COLUMN = 2
-DEPTH_CHUNKS = 4
-HIDDEN_TILES = 2
+DEPTH_PARTS = (1, 2, 1)
+DEPTH_CHUNKS = len(DEPTH_PARTS)
+HIDDEN_TILES = 1
 OUT_CHUNKS = 8
+Z_FIRST = 2
 
 
 def kernel(wide, x_hbm, gate_hbm, up_hbm, down_hbm, out_ref,
-           xg, gate, up, down, acc, peer, hid, own, y_out, y_in, z_out, z_in,
-           w_sem, d_sem, x_sem, zs, zr, ys, yr, ns, nr, rys, ryr, rzs, rzr):
+           xg, gate, up, down, acc, peer, hid, own, y_out, y_in, z_out, z_in, b_out, b_in, e_out, e_in,
+           w_sem, d_sem, x_sem, zs, zr, ys, yr, ns, nr, rys, ryr, rzs, rzr,
+           rbs, rbr, res, rer):
     zn = wide // COLUMN
     rows, width = x_hbm.shape
     half = zn * rows
     units = gate_hbm.shape[1]
-    depth = width // DEPTH_CHUNKS
+    unit = width // sum(DEPTH_PARTS)
     tile = units // HIDDEN_TILES
     cols = width // OUT_CHUNKS
 
@@ -34,8 +37,11 @@
     def along(d):
         return {"wide": lax.rem(z + d, zn) * COLUMN + y}
 
+    def span(k):
+        return pl.ds(sum(DEPTH_PARTS[:k]) * unit, DEPTH_PARTS[k] * unit)
+
     def local(k):
-        part = pl.ds(k * depth, depth)
+        part = span(k)
         return [
             pltpu.make_async_copy(gate_hbm.at[part], gate.at[part], w_sem.at[0, k]),
             pltpu.make_async_copy(up_hbm.at[part], up.at[part], w_sem.at[1, k]),
@@ -61,11 +67,11 @@
     pl.semaphore_wait(barrier, zn + 1)
 
     def z_copy(k, d):
-        part = pl.ds(k * depth, depth)
+        part = span(k)
         return remote(x_hbm.at[:, part], xg.at[zn - d, :, part], zs.at[k, d], zr.at[k, zn - d], along(d))
 
     def y_copy(k, s):
-        part = pl.ds(k * depth, depth)
+        part = span(k)
         src = x_hbm.at[:, part] if s == 0 else xg.at[s, :, part]
         return remote(src, xg.at[zn + s, :, part], ys.at[k, s], yr.at[k, s], across)
 
@@ -87,8 +93,8 @@
             y_copy(k, s).wait_recv()
         for copy in local(k):
             copy.wait()
-        part = pl.ds(k * depth, depth)
-        x = xg[:, :, part].reshape(2 * half, depth)
+        part = span(k)
+        x = xg[:, :, part].reshape(2 * half, DEPTH_PARTS[k] * unit)
         for t in range(HIDDEN_TILES):
             mid = pl.ds(t * tile, tile)
             for i, weight in enumerate((gate, up)):
@@ -122,13 +128,26 @@
     def rz_copy(n, d):
         return remote(z_out.at[n, d], z_in.at[n, zn - d], rzs.at[n, d], rzr.at[n, zn - d], along(d))
 
+    def rb_copy(n, d):
+        return remote(b_out.at[n, d], b_in.at[n, zn - d], rbs.at[n, d], rbr.at[n, zn - d], along(d))
+
+    def re_copy(n):
+        return remote(e_out.at[n], e_in.at[n], res.at[n], rer.at[n], across)
+
     for n in range(OUT_CHUNKS):
         products = jnp.dot(hid[...], down[:, pl.ds(n * cols, cols)], preferred_element_type=jnp.float32)
-        y_out[n] = products[half:].astype(jnp.bfloat16)
-        ry_copy(n).start()
-        own[n] = products[:half]
-
-    for n in range(OUT_CHUNKS):
+        if n < Z_FIRST:
+            blocks = products.reshape(2, zn, rows, cols)
+            for d in range(1, zn):
+                b_out[n, d] = blocks[:, d].astype(jnp.bfloat16)
+                rb_copy(n, d).start()
+            own[n, pl.ds(0, 2 * rows)] = blocks[:, 0].reshape(2 * rows, cols)
+        else:
+            y_out[n] = products[half:].astype(jnp.bfloat16)
+            ry_copy(n).start()
+            own[n] = products[:half]
+
+    for n in range(Z_FIRST, OUT_CHUNKS):
         ry_copy(n).wait_recv()
         for d in range(zn):
             row = pl.ds(d * rows, rows)
@@ -139,11 +158,24 @@
                 z_out[n, d] = value.astype(jnp.bfloat16)
                 rz_copy(n, d).start()
 
+    for n in range(Z_FIRST):
+        value = own[n, pl.ds(0, 2 * rows)]
+        for s in range(1, zn):
+            rb_copy(n, zn - s).wait_recv()
+            value = value + b_in[n, s].astype(jnp.float32).reshape(2 * rows, cols)
+        e_out[n] = value[rows:].astype(jnp.bfloat16)
+        re_copy(n).start()
+        own[n, pl.ds(0, rows)] = value[:rows]
+
     for n in range(OUT_CHUNKS):
         value = own[n, pl.ds(0, rows)]
-        for s in range(1, zn):
-            rz_copy(n, zn - s).wait_recv()
-            value = value + z_in[n, s].astype(jnp.float32)
+        if n < Z_FIRST:
+            re_copy(n).wait_recv()
+            value = value + e_in[n].astype(jnp.float32)
+        else:
+            for s in range(1, zn):
+                rz_copy(n, zn - s).wait_recv()
+                value = value + z_in[n, s].astype(jnp.float32)
         out_ref[:, pl.ds(n * cols, cols)] = value.astype(jnp.bfloat16)
 
     for k in range(DEPTH_CHUNKS):
@@ -154,9 +186,12 @@
     for t in range(HIDDEN_TILES):
         twin_copy(t).wait_send()
     for n in range(OUT_CHUNKS):
-        ry_copy(n).wait_send()
+        if n < Z_FIRST:
+            re_copy(n).wait_send()
+        else:
+            ry_copy(n).wait_send()
         for d in range(1, zn):
-            rz_copy(n, d).wait_send()
+            (rb_copy if n < Z_FIRST else rz_copy)(n, d).wait_send()
 
 
 def solution(mesh):
@@ -187,12 +222,18 @@
                 pltpu.VMEM((OUT_CHUNKS, half, cols), bf16),
                 pltpu.VMEM((OUT_CHUNKS, zn, rows, cols), bf16),
                 pltpu.VMEM((OUT_CHUNKS, zn, rows, cols), bf16),
+                pltpu.VMEM((max(Z_FIRST, 1), zn, 2, rows, cols), bf16),
+                pltpu.VMEM((max(Z_FIRST, 1), zn, 2, rows, cols), bf16),
+                pltpu.VMEM((max(Z_FIRST, 1), rows, cols), bf16),
+                pltpu.VMEM((max(Z_FIRST, 1), rows, cols), bf16),
                 dma((2, DEPTH_CHUNKS)), dma, dma,
                 dma((DEPTH_CHUNKS, zn)), dma((DEPTH_CHUNKS, zn)),
                 dma((DEPTH_CHUNKS, zn)), dma((DEPTH_CHUNKS, zn)),
                 dma((HIDDEN_TILES,)), dma((HIDDEN_TILES,)),
                 dma((OUT_CHUNKS,)), dma((OUT_CHUNKS,)),
                 dma((OUT_CHUNKS, zn)), dma((OUT_CHUNKS, zn)),
+                dma((max(Z_FIRST, 1), zn)), dma((max(Z_FIRST, 1), zn)),
+                dma((max(Z_FIRST, 1),)), dma((max(Z_FIRST, 1),)),
             ],
             compiler_params=pltpu.CompilerParams(
                 collective_id=0, has_side_effects=True, vmem_limit_bytes=56 * 1024 * 1024),

time: 45.2 us -> 42.2 us (0.934)
  Pallas kernels: 43.2 us -> 40.5 us
    pallas_call x1, Pallas kernels: 43.2 us -> 40.5 us  [body(): pl.pallas_call(functools.partial(kernel, wide), out_shape=jax.ShapeDtypeS...]
where the time goes in v2:
time: 42.2 us; the launch traced here: 42.1 us
  Pallas kernels  40.5 us (96%)
  local copies, waits for them, and re-layouts  1.57 us (4%)
    pallas_call x1, Pallas kernels, body(): pl.pallas_call(functools.partial(kernel, wide), out_shape=jax.ShapeDtypeS...  40.5 us
    unnamed x1, local copies, waits for them, and re-layouts  1.57 us

profile of v2, /device:TPU:1, one launch (start us, length us, event | category | flops | bytes accessed | tf_op | source)
XLA Modules:
  0.0 42.1 jit_solution(17960398174438887038)
XLA Ops:
  0.0 40.5 %shard_map.46 = bf16[16,4096]{1,0:T(8,128)(2,1)} custom-call(bf16[16,4096]{1,0:T(8,128)(2,1)} %x_hbm.1, bf16[4096,512]{1,0:T(8,128)(2,1)} %gate_hbm.1, bf16[4096,512]{1,0:T(8,128)(2,1)} %up_hbm.1, bf16[512,4096]{1,0:T(8,128)(2,1)} %down_hbm.1), custom_call_target="tpu_custom_call" | custom-call | tf_op jit(solution)/shard_map/pallas_call | solution.py:207
  40.5 1.6 %copy.6 = bf16[16,4096]{1,0:T(8,128)(2,1)} copy(bf16[16,4096]{1,0:T(8,128)(2,1)} %shard_map.46) | data formatting | bytes 262144

commit v3 on v2

--- a/solution.py
+++ b/solution.py
@@ -51,19 +51,18 @@
         return pltpu.make_async_remote_copy(
             src_ref=src, dst_ref=dst, send_sem=send, recv_sem=recv, device_id=to, device_id_type=MESH)
 
-    mine = pltpu.make_async_copy(x_hbm, xg.at[0], x_sem)
-    mine.start()
-    for k in range(DEPTH_CHUNKS):
-        for copy in local(k):
-            copy.start()
-    down_copy = pltpu.make_async_copy(down_hbm, down, d_sem)
-    down_copy.start()
-
     barrier = pltpu.get_barrier_semaphore()
     for d in range(1, zn):
         pl.semaphore_signal(barrier, inc=1, device_id=along(d), device_id_type=MESH)
     pl.semaphore_signal(barrier, inc=1, device_id=across, device_id_type=MESH)
     pl.semaphore_signal(barrier, inc=1, device_id=twin, device_id_type=MESH)
+    mine = pltpu.make_async_copy(x_hbm, xg.at[0], x_sem)
+    mine.start()
+    for k in range(DEPTH_CHUNKS):
+        for copy in local(k):
+            copy.start()
+    down_copy = pltpu.make_async_copy(down_hbm, down, d_sem)
+    down_copy.start()
     pl.semaphore_wait(barrier, zn + 1)
 
     def z_copy(k, d):
@@ -147,9 +146,17 @@
             ry_copy(n).start()
             own[n] = products[:half]
 
+    for k in range(DEPTH_CHUNKS):
+        for d in range(zn):
+            y_copy(k, d).wait_send()
+            if d > 0:
+                z_copy(k, d).wait_send()
+    for t in range(HIDDEN_TILES):
+        twin_copy(t).wait_send()
+
     for n in range(Z_FIRST, OUT_CHUNKS):
         ry_copy(n).wait_recv()
-        for d in range(zn):
+        for d in sorted(range(zn), key=lambda d: -min(d, zn - d)):
             row = pl.ds(d * rows, rows)
             value = own[n, row] + y_in[n, row].astype(jnp.float32)
             if d == 0:
@@ -178,13 +185,6 @@
                 value = value + z_in[n, s].astype(jnp.float32)
         out_ref[:, pl.ds(n * cols, cols)] = value.astype(jnp.bfloat16)
 
-    for k in range(DEPTH_CHUNKS):
-        for d in range(zn):
-            y_copy(k, d).wait_send()
-            if d > 0:
-                z_copy(k, d).wait_send()
-    for t in range(HIDDEN_TILES):
-        twin_copy(t).wait_send()
     for n in range(OUT_CHUNKS):
         if n < Z_FIRST:
             re_copy(n).wait_send()

time: 42.2 us -> 42.2 us (level)
  no operation moved by 1% of the time
where the time goes in v3:
time: 42.2 us; the launch traced here: 42 us
  Pallas kernels  40.5 us (96%)
  local copies, waits for them, and re-layouts  1.57 us (4%)
    pallas_call x1, Pallas kernels, body(): pl.pallas_call(functools.partial(kernel, wide), out_shape=jax.ShapeDtypeS...  40.5 us
    unnamed x1, local copies, waits for them, and re-layouts  1.57 us

profile of v3, /device:TPU:1, one launch (start us, length us, event | category | flops | bytes accessed | tf_op | source)
XLA Modules:
  0.0 42.0 jit_solution(7201971648292040785)
XLA Ops:
  0.0 40.5 %shard_map.46 = bf16[16,4096]{1,0:T(8,128)(2,1)} custom-call(bf16[16,4096]{1,0:T(8,128)(2,1)} %x_hbm.1, bf16[4096,512]{1,0:T(8,128)(2,1)} %gate_hbm.1, bf16[4096,512]{1,0:T(8,128)(2,1)} %up_hbm.1, bf16[512,4096]{1,0:T(8,128)(2,1)} %down_hbm.1), custom_call_target="tpu_custom_call" | custom-call | tf_op jit(solution)/shard_map/pallas_call | solution.py:207
  40.5 1.6 %copy.6 = bf16[16,4096]{1,0:T(8,128)(2,1)} copy(bf16[16,4096]{1,0:T(8,128)(2,1)} %shard_map.46) | data formatting | bytes 262144
